TPU v7x, 512 devices: a whole 4x4x16 slice. The times are simulated.
512 devices in a mesh: row: 4 (over x), col: 16 (over z), depth: 8 (over y, core).
Axes of the slice: x: 4, y: 4, z: 16, core: 2. Of those that a mesh axis runs over, the one named last changes fastest.
Arguments:
- x_blocks: bfloat16 [16384, 8, 2048], P('col', 'depth', 'row'), may hold values from -0.5 to 0.5
- cols_x: int32 [16, 8, 16], P('col', 'depth'), may hold values from 0 to 95, as said below
- s_blocks: bfloat16 [8, 4096, 4, 1024], P('depth', 'col', 'row'), may hold values from -0.8984375 to 0.8984375
- rows_s: int32 [8, 4, 32], P('depth', 'row'), may hold values from 0 to 95, as said below
- keep_mask: int32 [128, 4, 8], P('col', 'row', 'depth'), may hold values 0 or 1
Outputs:
- filtered: bfloat16 [16384, 4, 1024], P('col', 'row', 'depth')
Inputs may be any that keep to these rules, and one draw needn't show every extreme that they name: `cols_x`: within each list of 16 entries the numbers are distinct. `rows_s`: within each list of 32 entries the numbers are distinct.
All inputs are finite; a program needn't handle non-finite values. No bound on the sum of `keep_mask` on one device may be relied on, other than what follows from the above.
Results may differ from a plain program's by a relative error of at most 0.001.
Values may be sent and summed in bfloat16 or wider, within the bound.
A program may use at most 64 MiB of HBM per device.

v0:
```python
import functools

import jax
import jax.numpy as jnp
from jax import lax
from jax.experimental import pallas as pl
from jax.experimental.pallas import tpu as pltpu
from jax.sharding import PartitionSpec as P

BS = 128
TILE_ROWS = 256
TRAIL = 1
MESH = pl.DeviceIdType.MESH


def send_order():
    order = [(pair, 1) for pair in range(4)]
    for hop in range(2, 9 - TRAIL):
        order += [(0, hop), (1, hop)]
    for hop in range(2, 2 + TRAIL):
        order += [(0, hop + 7 - TRAIL), (1, hop + 7 - TRAIL), (2, hop)]
    for hop in range(2 + TRAIL, 9):
        order += [(2, hop), (3, hop - TRAIL)]
    order += [(3, hop) for hop in range(9 - TRAIL, 9)]
    return order


WORK = {
    (1, 3): ["x_forward"],
    (1, 6): ["x_ready"],
    (3, 2): ["land 0", "pick 0", "dot 0 0 2"],
    (2, 4): ["dot 0 2 2"],
    (3, 3): ["land 1", "pick 1", "dot 1 0 2"],
    (2, 5): ["dot 1 2 2", "share 0 0 4"],
    (3, 4): ["share 1 0 4"],
    (2, 8): ["pick 2", "dot 2 0 2", "dot 2 2 2"],
    (3, 7): ["share 2 0 2", "land 2", "pass", "share 2 2 2"],
    (3, 8): ["pick 3", "dot 3 0 2", "dot 3 2 2", "land 3", "late", "take", "finish"],
}


def kernel(sizes, x_in, s_in, cols, rows, mask, out, s_buf, x_buf, x_split, x_far, x_far_in, s_far_in, cur, sel, sel_last, oth, own, pair_in,
           red, pos, pos_last,           local_sem, s_send, s_recv, x_send, x_recv, p_send, p_recv, r_send, r_recv,
           f_send, f_recv):
    ring, wide, deep = sizes
    half_ring = ring // 2
    width_x, width_s = cols.shape[0], rows.shape[0]
    chips = deep // 2
    panel_rows = x_buf.shape[0]
    z, r, d = lax.axis_index("col"), lax.axis_index("row"), lax.axis_index("depth")
    y, core = lax.div(d, 2), lax.rem(d, 2)
    quarter = x_in.shape[1]
    half = quarter // 2
    z_to = (lax.rem(z + 1, ring), lax.rem(z + ring - 1, ring))
    r_to = (lax.rem(r + 1, wide), lax.rem(r + wide - 1, wide))
    partner = 2 * y + 1 - core
    far = lax.rem(z + half_ring, ring)

    barrier = pltpu.get_barrier_semaphore()
    friends = [{"col": z_to[0]}, {"col": z_to[1]}, {"row": r_to[0]}, {"row": r_to[1]}, {"depth": partner}]
    friends += [{"depth": 2 * lax.rem(y + j, chips) + core} for j in range(1, chips)]
    beside = (2 * lax.rem(y + 1, chips), 2 * lax.rem(y + chips - 1, chips) + 1)
    friends.append({"depth": jnp.where(core == 0, beside[1], beside[0])})
    for friend in friends:
        pl.semaphore_signal(barrier, inc=1, device_id=friend, device_id_type=MESH)
    pl.semaphore_wait(barrier, len(friends))

    def tile_of(pair, side):
        which = core if side else 1 - core
        step = (2, 3 - 2 * which, 1 + 2 * which, 0)[pair]
        return 2 * lax.rem(y + step, chips) + which

    def columns(pair, side):
        return pl.ds(pl.multiple_of(tile_of(pair, side) * BS, BS), BS)

    def s_copy(way, pair, side, hop):
        back = (hop - 1) if way == 1 else (ring - hop + 1)
        block = lax.rem(z + back, ring)
        tile = 2 * pair + side
        dst = s_buf.at[tile, block]
        src = s_in.at[:, columns(pair, side)] if hop == 1 else dst
        if hop == half_ring:
            src, dst = src.at[pl.ds(way * BS, BS)], dst.at[pl.ds(way * BS, BS)]
        return pltpu.make_async_remote_copy(
            src_ref=src, dst_ref=dst, send_sem=s_send.at[way, tile, hop - 1], recv_sem=s_recv.at[way, tile, hop - 1],
            device_id={"col": z_to[way]}, device_id_type=MESH)

    def x_copy(way, piece):
        if piece < 2:
            part = piece if way == 0 else 1 - piece
            owner = r
        else:
            part = way
            owner = r_to[1 - way]
        dst = x_buf.at[:, pl.ds(pl.multiple_of(owner * quarter + part * half, half), half)]
        src = x_in.at[:, pl.ds(part * half, half)] if piece < 2 else dst
        return pltpu.make_async_remote_copy(
            src_ref=src, dst_ref=dst, send_sem=x_send.at[way, piece], recv_sem=x_recv.at[way, piece],
            device_id={"row": r_to[way]}, device_id_type=MESH)

    def p_copy(pair, part):
        here = pl.ds(part * TILE_ROWS, TILE_ROWS)
        return pltpu.make_async_remote_copy(
            src_ref=oth.at[pair, here], dst_ref=pair_in.at[pair, here], send_sem=p_send.at[pair, part],
            recv_sem=p_recv.at[pair, part], device_id={"depth": partner}, device_id_type=MESH)

    def r_copy(pair, part):
        here = pl.ds(part * TILE_ROWS, TILE_ROWS)
        return pltpu.make_async_remote_copy(
            src_ref=own.at[pair, here], dst_ref=red.at[pair, here], send_sem=r_send.at[pair, part],
            recv_sem=r_recv.at[pair, part], device_id={"depth": tile_of(pair, 1)}, device_id_type=MESH)

    def f_copy(which, sender, kind):
        side = jnp.where(core == which, 1, 0)
        src, dst = (x_far, x_far_in.at[sender]) if kind == 0 else (s_buf.at[4 + side, far], s_far_in.at[sender])
        return pltpu.make_async_remote_copy(
            src_ref=src, dst_ref=dst, send_sem=f_send.at[kind, which], recv_sem=f_recv.at[kind, sender],
            device_id={"depth": beside[which]}, device_id_type=MESH)

    started = []

    def start(copy):
        copy.start()
        started.append(copy)

    def advance(pair, hop):
        for side in range(2):
            for way in range(2):
                if hop > 1:
                    s_copy(way, pair, side, hop - 1).wait_recv()
                if hop <= half_ring:
                    start(s_copy(way, pair, side, hop))

    parts = panel_rows // TILE_ROWS
    last = chips - 1
    late_from = chips - 2

    def stage(pair, block):
        for side in range(2):
            for i in range(2):
                cur[side, 2 * block + i] = s_buf[2 * pair + side, block, pl.ds(i * BS, BS), :]

    def pick(pair):
        for back in range(ring):
            if pair >= late_from and back == half_ring:
                for side in range(2):
                    for i in range(2):
                        cur[side, 2 * far + i] = jnp.zeros((BS, BS), cur.dtype)
            else:
                stage(pair, lax.rem(z + back, ring))
        for a in range(width_x):
            at = pos[a]
            for side in range(2):
                sel[a * BS:(a + 1) * BS, side * BS:(side + 1) * BS] = cur[side, at]

    def dot(pair, part, count):
        here = pl.ds(part * TILE_ROWS, count * TILE_ROWS)
        value = jnp.dot(x_buf[here, :], sel[...], preferred_element_type=jnp.float32)
        oth[pair, here, :] = value[:, :BS]
        if pair != last:
            for k in range(part, part + count):
                start(p_copy(pair, k))
        own[pair, here, :] = value[:, BS:]

    def late():
        stage(last, far)
        for i in range(2):
            at = pos_last[2 + i]
            for side in range(2):
                sel_last[i * BS:(i + 1) * BS, side * BS:(side + 1) * BS] = cur[side, at]
        for part in range(parts):
            here = pl.ds(part * TILE_ROWS, TILE_ROWS)
            value = jnp.dot(x_far[here, :], sel_last[...], preferred_element_type=jnp.float32)
            oth[last, here, :] = oth[last, here, :] + value[:, :BS]
            start(p_copy(last, part))
            own[last, here, :] = own[last, here, :] + value[:, BS:]

    def pass_on():
        for which in range(2):
            start(f_copy(which, core, 1))

    def take():
        for kind in range(2):
            for sender in range(2):
                f_copy(0, sender, kind).wait_recv()
        for part in range(parts):
            here = pl.ds(part * TILE_ROWS, TILE_ROWS)
            value = own[last, here, :]
            for sender in range(2):
                value = value + jnp.dot(x_far_in[sender, here, :], s_far_in[sender], preferred_element_type=jnp.float32)
            own[last, here, :] = value

    def share(pair, first, count):
        for part in range(first, first + count):
            here = pl.ds(part * TILE_ROWS, TILE_ROWS)
            p_copy(pair, part).wait_recv()
            own[pair, here, :] = own[pair, here, :] + pair_in[pair, here, :]
            start(r_copy(pair, part))

    def finish():
        for part in range(parts):
            for pair in range(last):
                r_copy(pair, part).wait_recv()
            p_copy(last, part).wait_recv()
            for i in range(part * TILE_ROWS // BS, (part + 1) * TILE_ROWS // BS):
                here = pl.ds(i * BS, BS)
                value = own[last, here, :] + pair_in[last, here, :]
                for pair in range(last):
                    value = value + red[pair, here, :]
                out[here, :] = jnp.where(mask[i] > 0, value, 0.0).astype(out.dtype)

    def x_forward():
        for way in range(2):
            x_copy(way, 0).wait_recv()
            start(x_copy(way, 2))

    def x_ready():
        for way in range(2):
            for piece in (1, 2):
                x_copy(way, piece).wait_recv()
        for a in range(width_x):
            x_split[a] = x_buf[:, a * BS:(a + 1) * BS]
        x_split[width_x] = jnp.zeros((panel_rows, BS), x_split.dtype)
        for i in range(2):
            x_far[:, i * BS:(i + 1) * BS] = x_split[pos_last[i]]
        for which in range(2):
            start(f_copy(which, core, 0))

    local_copies = [pltpu.make_async_copy(
        x_in, x_buf.at[:, pl.ds(pl.multiple_of(r * quarter, quarter), quarter)], local_sem.at[0])]
    for pair in range(chips):
        for side in range(2):
            local_copies.append(pltpu.make_async_copy(
                s_in.at[:, columns(pair, side)], s_buf.at[2 * pair + side, z], local_sem.at[1 + 2 * pair + side]))

    def find(a, carry):
        wanted = cols[a]
        at = jnp.int32(width_s)
        for q in range(width_s):
            at = jnp.where(rows[q] == wanted, jnp.int32(q), at)
        pos[a] = at
        return carry

    def find_last(i, carry):
        wanted = rows[2 * far + i]
        at_x, at_s = jnp.int32(width_x), jnp.int32(width_s)
        for a in range(width_x):
            same = cols[a] == wanted
            at_x = jnp.where(same, jnp.int32(a), at_x)
            at_s = jnp.where(same, 2 * far + i, at_s)
        pos_last[i] = at_x
        pos_last[2 + i] = at_s
        return carry

    order = send_order()
    for pair, hop in order[:1]:
        advance(pair, hop)
    for way in range(2):
        start(x_copy(way, 0))
    for pair, hop in order[1:chips]:
        advance(pair, hop)
    for way in range(2):
        start(x_copy(way, 1))
    for copy in local_copies:
        copy.start()
    for side in range(2):
        cur[side, width_s] = jnp.zeros((BS, BS), cur.dtype)
    lax.fori_loop(0, width_x, find, 0)
    lax.fori_loop(0, 2, find_last, 0)
    for copy in local_copies:
        copy.wait()

    steps = {"x_forward": x_forward, "x_ready": x_ready, "pick": pick, "dot": dot, "share": share, "late": late, "pass": pass_on,
             "take": take, "finish": finish,
             "land": lambda pair: advance(pair, half_ring + 1)}
    for pair, hop in order[chips:]:
        advance(pair, hop)
        for item in WORK.get((pair, hop), []):
            name, *numbers = item.split()
            steps[name](*map(int, numbers))
    for copy in started:
        copy.wait_send()


def on_device(sizes, x_blocks, cols_x, s_blocks, rows_s, keep_mask):
    ring, wide, deep = sizes
    panel_rows, quarter = x_blocks.shape[0], x_blocks.shape[2]
    own_rows, kept = s_blocks.shape[1], s_blocks.shape[3]
    width_x, width_s = cols_x.shape[2], rows_s.shape[2]
    chips = deep // 2
    parts = panel_rows // TILE_ROWS
    dma = pltpu.SemaphoreType.DMA
    smem = pl.BlockSpec(memory_space=pltpu.SMEM)
    anywhere = pl.BlockSpec(memory_space=pl.ANY)
    result = pl.pallas_call(
        functools.partial(kernel, sizes),
        out_shape=jax.ShapeDtypeStruct((panel_rows, BS), jnp.bfloat16),
        in_specs=[anywhere, anywhere, smem, smem, smem],
        out_specs=pl.BlockSpec(memory_space=pltpu.VMEM),
        scratch_shapes=[
            pltpu.VMEM((deep, ring, own_rows, BS), jnp.bfloat16),
            pltpu.VMEM((panel_rows, quarter * wide), jnp.bfloat16),
            pltpu.VMEM((width_x + 1, panel_rows, BS), jnp.bfloat16),
            pltpu.VMEM((panel_rows, 2 * BS), jnp.bfloat16),
            pltpu.VMEM((2, panel_rows, 2 * BS), jnp.bfloat16),
            pltpu.VMEM((2, own_rows, BS), jnp.bfloat16),
            pltpu.VMEM((2, width_s + 1, BS, BS), jnp.bfloat16),
            pltpu.VMEM((width_x * BS, 2 * BS), jnp.bfloat16),
            pltpu.VMEM((2 * BS, 2 * BS), jnp.bfloat16),
            pltpu.VMEM((chips, panel_rows, BS), jnp.float32),
            pltpu.VMEM((chips, panel_rows, BS), jnp.float32),
            pltpu.VMEM((chips, panel_rows, BS), jnp.float32),
            pltpu.VMEM((chips - 1, panel_rows, BS), jnp.float32),
            pltpu.SMEM((width_x,), jnp.int32),
            pltpu.SMEM((4,), jnp.int32),
            dma((1 + deep,)),
            dma((2, deep, ring // 2)),
            dma((2, deep, ring // 2)),
            dma((2, 3)),
            dma((2, 3)),
            dma((chips, parts)),
            dma((chips, parts)),
            dma((chips - 1, parts)),
            dma((chips - 1, parts)),
            dma((2, 2)),
            dma((2, 2)),
        ],
        compiler_params=pltpu.CompilerParams(collective_id=0, has_side_effects=True, vmem_limit_bytes=213 << 18),
    )(
        x_blocks.reshape(panel_rows, quarter),
        s_blocks.reshape(own_rows, kept),
        cols_x.reshape(width_x),
        rows_s.reshape(width_s),
        keep_mask.reshape(keep_mask.shape[0]),
    )
    return result.reshape(panel_rows, 1, BS)


def solution(mesh):
    sizes = (mesh.shape["col"], mesh.shape["row"], mesh.shape["depth"])
    placed = (
        P("col", "depth", "row"),
        P("col", "depth", None),
        P("depth", "col", "row", None),
        P("depth", "row", None),
        P("col", "row", "depth"),
    )
    return jax.shard_map(
        functools.partial(on_device, sizes), mesh=mesh, in_specs=placed, out_specs=P("col", "row", "depth"), check_vma=False
    )
```

profile of v0, /device:TPU:1, one launch (start us, length us, event | category | flops | bytes accessed | tf_op | source)
XLA Modules:
  0.0 110.4 jit_solution(3479830168479540907)
XLA Ops:
  0.0 0.0 copy-start
  0.0 0.0 copy-start.1
  0.0 0.0 copy-start.2
  0.0 0.6 copy-done
  0.7 0.0 copy-done.1
  0.7 0.0 copy-done.2
  0.7 108.9 %shard_map.55 = bf16[1024,128]{1,0:T(8,128)(2,1)S(1)} custom-call(bf16[1024,512]{1,0:T(8,128)(2,1)} %bitcast.10, bf16[256,1024]{1,0:T(8,128)(2,1)} %bitcast.11, s32[16]{0:T(128)S(1)} %bitcast.7, s32[32]{0:T(128)S(1)} %bitcast.8, s32[8]{0:T(128)S(1)} %bitcast.9), custom_call_target="tpu_custom_call" | custom-call | tf_op jit(solution)/shard_map/pallas_call | solution.py:295
  109.6 0.7 copy.7
Async XLA Ops:
  0.0 0.7 copy-start
  0.0 0.7 copy-start.1
  0.0 0.7 copy-start.2
where the time goes:
time: 110 us
  Pallas kernels  109 us (99%)
  local copies, waits for them, and re-layouts  1.39 us (1%)
    pallas_call x1, Pallas kernels, on_device(): pl.pallas_call(functools.partial(kernel, sizes), out_shape=jax.ShapeDtype...  109 us

commit v1 on v0

--- a/solution.py
+++ b/solution.py
@@ -39,8 +39,8 @@
 }
 
 
-def kernel(sizes, x_in, s_in, cols, rows, mask, out, s_buf, x_buf, x_split, x_far, x_far_in, s_far_in, cur, sel, sel_last, oth, own, pair_in,
-           red, pos, pos_last,           local_sem, s_send, s_recv, x_send, x_recv, p_send, p_recv, r_send, r_recv,
+def kernel(sizes, x_in, s_in, cols_in, rows_in, mask_in, out, cols, rows, mask, s_buf, x_buf, x_split, x_far, x_far_in, s_far_in, cur, sel, oth, own, pair_in,
+           red, pos, pos_far,           local_sem, s_send, s_recv, x_send, x_recv, p_send, p_recv, r_send, r_recv,
            f_send, f_recv):
     ring, wide, deep = sizes
     half_ring = ring // 2
@@ -112,7 +112,8 @@
 
     def f_copy(which, sender, kind):
         side = jnp.where(core == which, 1, 0)
-        src, dst = (x_far, x_far_in.at[sender]) if kind == 0 else (s_buf.at[4 + side, far], s_far_in.at[sender])
+        place = pl.ds(pl.multiple_of(sender * 2 * BS, 2 * BS), 2 * BS)
+        src, dst = (x_far, x_far_in.at[:, place]) if kind == 0 else (s_buf.at[4 + side, far], s_far_in.at[place])
         return pltpu.make_async_remote_copy(
             src_ref=src, dst_ref=dst, send_sem=f_send.at[kind, which], recv_sem=f_recv.at[kind, sender],
             device_id={"depth": beside[which]}, device_id_type=MESH)
@@ -163,14 +164,10 @@
         own[pair, here, :] = value[:, BS:]
 
     def late():
-        stage(last, far)
-        for i in range(2):
-            at = pos_last[2 + i]
-            for side in range(2):
-                sel_last[i * BS:(i + 1) * BS, side * BS:(side + 1) * BS] = cur[side, at]
+        rows_far = jnp.concatenate([s_buf[2 * last, far], s_buf[2 * last + 1, far]], axis=1)
         for part in range(parts):
             here = pl.ds(part * TILE_ROWS, TILE_ROWS)
-            value = jnp.dot(x_far[here, :], sel_last[...], preferred_element_type=jnp.float32)
+            value = jnp.dot(x_far[here, :], rows_far, preferred_element_type=jnp.float32)
             oth[last, here, :] = oth[last, here, :] + value[:, :BS]
             start(p_copy(last, part))
             own[last, here, :] = own[last, here, :] + value[:, BS:]
@@ -183,12 +180,10 @@
         for kind in range(2):
             for sender in range(2):
                 f_copy(0, sender, kind).wait_recv()
-        for part in range(parts):
-            here = pl.ds(part * TILE_ROWS, TILE_ROWS)
-            value = own[last, here, :]
-            for sender in range(2):
-                value = value + jnp.dot(x_far_in[sender, here, :], s_far_in[sender], preferred_element_type=jnp.float32)
-            own[last, here, :] = value
+        for part in range(0, parts, 2):
+            here = pl.ds(part * TILE_ROWS, 2 * TILE_ROWS)
+            value = jnp.dot(x_far_in[here, :], s_far_in[...], preferred_element_type=jnp.float32)
+            own[last, here, :] = own[last, here, :] + value
 
     def share(pair, first, count):
         for part in range(first, first + count):
@@ -222,7 +217,7 @@
             x_split[a] = x_buf[:, a * BS:(a + 1) * BS]
         x_split[width_x] = jnp.zeros((panel_rows, BS), x_split.dtype)
         for i in range(2):
-            x_far[:, i * BS:(i + 1) * BS] = x_split[pos_last[i]]
+            x_far[:, i * BS:(i + 1) * BS] = x_split[pos_far[i]]
         for which in range(2):
             start(f_copy(which, core, 0))
 
@@ -232,6 +227,9 @@
         for side in range(2):
             local_copies.append(pltpu.make_async_copy(
                 s_in.at[:, columns(pair, side)], s_buf.at[2 * pair + side, z], local_sem.at[1 + 2 * pair + side]))
+
+    for k, (src, dst) in enumerate(((cols_in, cols), (rows_in, rows), (mask_in, mask))):
+        local_copies.append(pltpu.make_async_copy(src, dst, local_sem.at[1 + deep + k]))
 
     def find(a, carry):
         wanted = cols[a]
@@ -241,15 +239,12 @@
         pos[a] = at
         return carry
 
-    def find_last(i, carry):
+    def find_far(i, carry):
         wanted = rows[2 * far + i]
-        at_x, at_s = jnp.int32(width_x), jnp.int32(width_s)
+        at = jnp.int32(width_x)
         for a in range(width_x):
-            same = cols[a] == wanted
-            at_x = jnp.where(same, jnp.int32(a), at_x)
-            at_s = jnp.where(same, 2 * far + i, at_s)
-        pos_last[i] = at_x
-        pos_last[2 + i] = at_s
+            at = jnp.where(cols[a] == wanted, jnp.int32(a), at)
+        pos_far[i] = at
         return carry
 
     order = send_order()
@@ -265,10 +260,10 @@
         copy.start()
     for side in range(2):
         cur[side, width_s] = jnp.zeros((BS, BS), cur.dtype)
-    lax.fori_loop(0, width_x, find, 0)
-    lax.fori_loop(0, 2, find_last, 0)
     for copy in local_copies:
         copy.wait()
+    lax.fori_loop(0, width_x, find, 0)
+    lax.fori_loop(0, 2, find_far, 0)
 
     steps = {"x_forward": x_forward, "x_ready": x_ready, "pick": pick, "dot": dot, "share": share, "late": late, "pass": pass_on,
              "take": take, "finish": finish,
@@ -290,30 +285,31 @@
     chips = deep // 2
     parts = panel_rows // TILE_ROWS
     dma = pltpu.SemaphoreType.DMA
-    smem = pl.BlockSpec(memory_space=pltpu.SMEM)
     anywhere = pl.BlockSpec(memory_space=pl.ANY)
     result = pl.pallas_call(
         functools.partial(kernel, sizes),
         out_shape=jax.ShapeDtypeStruct((panel_rows, BS), jnp.bfloat16),
-        in_specs=[anywhere, anywhere, smem, smem, smem],
+        in_specs=[anywhere] * 5,
         out_specs=pl.BlockSpec(memory_space=pltpu.VMEM),
         scratch_shapes=[
+            pltpu.SMEM((width_x,), jnp.int32),
+            pltpu.SMEM((width_s,), jnp.int32),
+            pltpu.SMEM((keep_mask.shape[0],), jnp.int32),
             pltpu.VMEM((deep, ring, own_rows, BS), jnp.bfloat16),
             pltpu.VMEM((panel_rows, quarter * wide), jnp.bfloat16),
             pltpu.VMEM((width_x + 1, panel_rows, BS), jnp.bfloat16),
             pltpu.VMEM((panel_rows, 2 * BS), jnp.bfloat16),
-            pltpu.VMEM((2, panel_rows, 2 * BS), jnp.bfloat16),
-            pltpu.VMEM((2, own_rows, BS), jnp.bfloat16),
+            pltpu.VMEM((panel_rows, 4 * BS), jnp.bfloat16),
+            pltpu.VMEM((4 * BS, BS), jnp.bfloat16),
             pltpu.VMEM((2, width_s + 1, BS, BS), jnp.bfloat16),
             pltpu.VMEM((width_x * BS, 2 * BS), jnp.bfloat16),
-            pltpu.VMEM((2 * BS, 2 * BS), jnp.bfloat16),
             pltpu.VMEM((chips, panel_rows, BS), jnp.float32),
             pltpu.VMEM((chips, panel_rows, BS), jnp.float32),
             pltpu.VMEM((chips, panel_rows, BS), jnp.float32),
             pltpu.VMEM((chips - 1, panel_rows, BS), jnp.float32),
             pltpu.SMEM((width_x,), jnp.int32),
-            pltpu.SMEM((4,), jnp.int32),
-            dma((1 + deep,)),
+            pltpu.SMEM((2,), jnp.int32),
+            dma((4 + deep,)),
             dma((2, deep, ring // 2)),
             dma((2, deep, ring // 2)),
             dma((2, 3)),

time: 110 us -> 110 us (level)
  no operation moved by 1% of the time
where the time goes in v1:
time: 110 us
  Pallas kernels  108 us (98%)
  local copies, waits for them, and re-layouts  1.39 us (1%)
    pallas_call x1, Pallas kernels, on_device(): pl.pallas_call(functools.partial(kernel, sizes), out_shape=jax.ShapeDtype...  108 us

profile of v1, /device:TPU:1, one launch (start us, length us, event | category | flops | bytes accessed | tf_op | source)
XLA Modules:
  0.0 109.7 jit_solution(8259413119586008590)
XLA Ops:
  0.0 0.0 copy-start
  0.0 0.0 copy-start.1
  0.0 0.0 copy-start.2
  0.0 0.6 copy-done
  0.7 0.0 copy-done.1
  0.7 0.0 copy-done.2
  0.7 108.3 %shard_map.55 = bf16[1024,128]{1,0:T(8,128)(2,1)S(1)} custom-call(bf16[1024,512]{1,0:T(8,128)(2,1)} %bitcast.10, bf16[256,1024]{1,0:T(8,128)(2,1)} %bitcast.11, s32[16]{0:T(128)S(1)} %bitcast.7, s32[32]{0:T(128)S(1)} %bitcast.8, s32[8]{0:T(128)S(1)} %bitcast.9), custom_call_target="tpu_custom_call" | custom-call | tf_op jit(solution)/shard_map/pallas_call | solution.py:289
  109.0 0.7 copy.7
Async XLA Ops:
  0.0 0.7 copy-start
  0.0 0.7 copy-start.1
  0.0 0.7 copy-start.2

commit v2 on v1

--- a/solution.py
+++ b/solution.py
@@ -26,8 +26,8 @@
 
 
 WORK = {
-    (1, 3): ["x_forward"],
-    (1, 6): ["x_ready"],
+    (1, 4): ["x_forward"],
+    (1, 7): ["x_ready"],
     (3, 2): ["land 0", "pick 0", "dot 0 0 2"],
     (2, 4): ["dot 0 2 2"],
     (3, 3): ["land 1", "pick 1", "dot 1 0 2"],
@@ -35,7 +35,7 @@
     (3, 4): ["share 1 0 4"],
     (2, 8): ["pick 2", "dot 2 0 2", "dot 2 2 2"],
     (3, 7): ["share 2 0 2", "land 2", "pass", "share 2 2 2"],
-    (3, 8): ["pick 3", "dot 3 0 2", "dot 3 2 2", "land 3", "late", "take", "finish"],
+    (3, 8): ["pick 3", "dot 3 0 2", "dot 3 2 2", "gather", "land 3", "late", "take", "finish"],
 }
 
 
@@ -176,6 +176,15 @@
         for which in range(2):
             start(f_copy(which, core, 1))
 
+    def gather():
+        for part in range(parts):
+            here = pl.ds(part * TILE_ROWS, TILE_ROWS)
+            value = own[last, here, :]
+            for pair in range(last - 1):
+                r_copy(pair, part).wait_recv()
+                value = value + red[pair, here, :]
+            own[last, here, :] = value
+
     def take():
         for kind in range(2):
             for sender in range(2):
@@ -194,14 +203,12 @@
 
     def finish():
         for part in range(parts):
-            for pair in range(last):
-                r_copy(pair, part).wait_recv()
+            r_copy(last - 1, part).wait_recv()
             p_copy(last, part).wait_recv()
             for i in range(part * TILE_ROWS // BS, (part + 1) * TILE_ROWS // BS):
                 here = pl.ds(i * BS, BS)
                 value = own[last, here, :] + pair_in[last, here, :]
-                for pair in range(last):
-                    value = value + red[pair, here, :]
+                value = value + red[last - 1, here, :]
                 out[here, :] = jnp.where(mask[i] > 0, value, 0.0).astype(out.dtype)
 
     def x_forward():
@@ -266,7 +273,7 @@
     lax.fori_loop(0, 2, find_far, 0)
 
     steps = {"x_forward": x_forward, "x_ready": x_ready, "pick": pick, "dot": dot, "share": share, "late": late, "pass": pass_on,
-             "take": take, "finish": finish,
+             "take": take, "gather": gather, "finish": finish,
              "land": lambda pair: advance(pair, half_ring + 1)}
     for pair, hop in order[chips:]:
         advance(pair, hop)

time: 110 us -> 110 us (level)
  no operation moved by 1% of the time
where the time goes in v2:
time: 110 us
  Pallas kernels  108 us (98%)
  local copies, waits for them, and re-layouts  1.39 us (1%)
    pallas_call x1, Pallas kernels, on_device(): pl.pallas_call(functools.partial(kernel, sizes), out_shape=jax.ShapeDtype...  108 us

profile of v2, /device:TPU:1, one launch (start us, length us, event | category | flops | bytes accessed | tf_op | source)
XLA Modules:
  0.0 109.7 jit_solution(5088805370372877219)
XLA Ops:
  0.0 0.0 copy-start
  0.0 0.0 copy-start.1
  0.0 0.0 copy-start.2
  0.0 0.6 copy-done
  0.7 0.0 copy-done.1
  0.7 0.0 copy-done.2
  0.7 108.3 %shard_map.55 = bf16[1024,128]{1,0:T(8,128)(2,1)S(1)} custom-call(bf16[1024,512]{1,0:T(8,128)(2,1)} %bitcast.10, bf16[256,1024]{1,0:T(8,128)(2,1)} %bitcast.11, s32[16]{0:T(128)S(1)} %bitcast.7, s32[32]{0:T(128)S(1)} %bitcast.8, s32[8]{0:T(128)S(1)} %bitcast.9), custom_call_target="tpu_custom_call" | custom-call | tf_op jit(solution)/shard_map/pallas_call | solution.py:296
  109.0 0.7 copy.7
Async XLA Ops:
  0.0 0.7 copy-start
  0.0 0.7 copy-start.1
  0.0 0.7 copy-start.2

commit v3 on v2

--- a/solution.py
+++ b/solution.py
@@ -33,9 +33,9 @@
     (3, 3): ["land 1", "pick 1", "dot 1 0 2"],
     (2, 5): ["dot 1 2 2", "share 0 0 4"],
     (3, 4): ["share 1 0 4"],
-    (2, 8): ["pick 2", "dot 2 0 2", "dot 2 2 2"],
+    (2, 8): ["pick 2", "dot 2 0 4"],
     (3, 7): ["share 2 0 2", "land 2", "pass", "share 2 2 2"],
-    (3, 8): ["pick 3", "dot 3 0 2", "dot 3 2 2", "gather", "land 3", "late", "take", "finish"],
+    (3, 8): ["pick 3", "dot 3 0 4", "gather", "land 3", "late", "take", "finish"],
 }
 
 

time: 110 us -> 110 us (level)
  no operation moved by 1% of the time
where the time goes in v3:
time: 110 us
  Pallas kernels  109 us (99%)
  local copies, waits for them, and re-layouts  1.39 us (1%)
    pallas_call x1, Pallas kernels, on_device(): pl.pallas_call(functools.partial(kernel, sizes), out_shape=jax.ShapeDtype...  109 us

profile of v3, /device:TPU:1, one launch (start us, length us, event | category | flops | bytes accessed | tf_op | source)
XLA Modules:
  0.0 110.1 jit_solution(6292928225863070068)
XLA Ops:
  0.0 0.0 copy-start
  0.0 0.0 copy-start.1
  0.0 0.0 copy-start.2
  0.0 0.6 copy-done
  0.7 0.0 copy-done.1
  0.7 0.0 copy-done.2
  0.7 108.7 %shard_map.55 = bf16[1024,128]{1,0:T(8,128)(2,1)S(1)} custom-call(bf16[1024,512]{1,0:T(8,128)(2,1)} %bitcast.10, bf16[256,1024]{1,0:T(8,128)(2,1)} %bitcast.11, s32[16]{0:T(128)S(1)} %bitcast.7, s32[32]{0:T(128)S(1)} %bitcast.8, s32[8]{0:T(128)S(1)} %bitcast.9), custom_call_target="tpu_custom_call" | custom-call | tf_op jit(solution)/shard_map/pallas_call | solution.py:296
  109.4 0.7 copy.7
Async XLA Ops:
  0.0 0.7 copy-start
  0.0 0.7 copy-start.1
  0.0 0.7 copy-start.2
